TPU v7x, 32 devices: a whole 2x2x4 slice. The times are simulated.
32 devices in a mesh: row: 4 (over x, core), col: 8 (over z, y).
Axes of the slice: x: 2, y: 2, z: 4, core: 2. Of those that a mesh axis runs over, the one named last changes fastest.
Arguments:
- a_blocks: float32 [4, 8, 2, 2, 128, 128], P('row', 'col'), may hold values from -0.5 to 0.5
- a_rows: int32 [4, 8, 2, 2], P('row', 'col'), may hold values from 0 to 3, as said below
- b_blocks: float32 [4, 8, 2, 4, 128, 128], P('row', 'col'), may hold values from -6 to 6
- send_list: int32 [4, 8, 2, 4, 2], P('row', 'col'), may hold values from -1 to 3, as said below
- c_partial: float32 [4, 8, 4, 128, 128], P('row', 'col'), may hold values from -6 to 6
- c_list: int32 [4, 8, 4], P('row', 'col'), may hold values from 0 to 7, as said below
Outputs:
- c_blocks: float32 [4, 8, 4, 128, 128], P('row', 'col')
Inputs may be any that keep to these rules, and one draw needn't show every extreme that they name: The 2 entries of a_rows for one device and one section are distinct. `send_list`: each list holds 1 to 2 distinct block numbers first, then -1 in the rest of its slots. `c_list`: the 4 entries of a device are distinct.
All inputs are finite; a program needn't handle non-finite values.
Results may differ from a plain program's by a relative error of at most 0.0003.
Values sent between devices are 32-bit elements; how exact they have to be, the bound alone decides.
A program may use at most 64 MiB of HBM per device.

v0:
```python
import jax
import jax.numpy as jnp
from jax import lax
from jax.sharding import PartitionSpec as P

BS = 128
SECTIONS = 2
RB = 4
CB = 2


def accumulate(running, blocks, slot_lists, row_panel, panel_rows, per_row):
    piece_rows = slot_lists.shape[0]
    source = jnp.arange(piece_rows, dtype=jnp.int32)[:, None]
    entry = jnp.maximum(slot_lists, 0)
    inner = source * per_row + entry // CB
    column = entry % CB
    a_chosen = row_panel[inner]
    block_rows = panel_rows[inner]
    products = jnp.einsum(
        "qtnxy,qtyz->qtnxz",
        a_chosen,
        blocks,
        precision=lax.Precision.HIGHEST,
        preferred_element_type=jnp.float32,
    )
    target = block_rows * CB + column[:, :, None]
    onehot = (target[..., None] == jnp.arange(RB * CB, dtype=jnp.int32)).astype(jnp.float32)
    return running + jnp.einsum(
        "qtnc,qtnxz->cxz",
        onehot,
        products,
        precision=lax.Precision.HIGHEST,
        preferred_element_type=jnp.float32,
    )


def body(a_blocks, a_rows, b_blocks, send_list, c_partial, c_list):
    row_count = lax.axis_size("row")
    col_count = lax.axis_size("col")
    per_row = col_count // row_count
    running = jnp.zeros((RB * CB, BS, BS), jnp.float32)
    for section_index in range(SECTIONS):
        row_panel, panel_rows = (
            lax.all_gather(a_blocks[0, :, section_index], "col", axis=0, tiled=True),
            lax.all_gather(a_rows[0, :, section_index], "col", axis=0, tiled=True),
        )
        arrived_lists = lax.all_to_all(
            send_list[0, 0, section_index], "row", split_axis=0, concat_axis=0, tiled=True
        )
        shards = lax.all_gather(b_blocks[:, 0, section_index], "row", axis=0, tiled=True)
        piece_rows = shards.shape[0]
        picker = jnp.arange(piece_rows, dtype=jnp.int32)[:, None]
        chosen = shards[picker, jnp.maximum(arrived_lists, 0)]
        chosen = jnp.where((arrived_lists >= 0)[:, :, None, None], chosen, jnp.zeros_like(chosen))
        running = accumulate(running, chosen, arrived_lists, row_panel, panel_rows, per_row)
    result = c_partial[0, 0] + running[c_list[0, 0]]
    return result[None, None]


def solution(mesh):
    placed = (
        P("row", "col", None, None, None, None),
        P("row", "col", None, None),
        P("row", "col", None, None, None, None),
        P("row", "col", None, None, None),
        P("row", "col", None, None, None),
        P("row", "col", None),
    )
    return jax.shard_map(
        body,
        mesh=mesh,
        in_specs=placed,
        out_specs=P("row", "col", None, None, None),
        check_vma=False,
    )
```

profile of v0, /device:TPU:0, one launch (start us, length us, event | category | flops | bytes accessed | tf_op | source)
XLA Modules:
  0.0 145.6 jit_solution(4943668316628235160)
XLA Ops:
  6.5 1.9 %fusion.26 = (f32[1,1,1,4,128,128]{5,4,3,2,1,0:T(8,128)}, f32[1,1,1,4,128,128]{5,4,3,2,1,0:T(8,128)}) fusion(f32[1,1,2,4,128,128]{5,4,3,2,1,0:T(8,128)} %param.8), kind=kLoop, calls=%fused_computation.64 | loop fusion | bytes 1048576 | tf_op jit(solution)/shard_map/slice | solution.py:51
  8.5 0.7 all-gather.13.cloned.1.call-update
  9.2 0.1 copy-done.1
  9.3 0.7 fusion.27
  10.1 0.7 copy-done.2
  10.8 0.7 copy.105
  11.4 4.2 %all-to-all-start = ((s32[4,1,2]{2,1,0:T(1,128)}), s32[4,1,2]{2,1,0:T(1,128)S(1)}, u32[]{:S(2)}, u32[]{:S(2)}) async-start(s32[4,1,2]{2,1,0:T(1,128)} %copy.105), calls=%async_computation | async-start | bytes 4096 | tf_op jit(solution)/shard_map/all_to_all | solution.py:48
  15.6 0.6 all-gather.11.cloned.1.call-update
  16.2 0.7 copy.119
  16.9 21.2 %all-gather.3 = s32[8,1,1,2]{3,2,1,0:T(1,128)S(1)} all-gather(s32[1,1,1,2]{3,2,1,0:T(1,128)S(1)} %get-tuple-element.12), channel_id=5, replica_groups=mesh['row'=4,'col'=8] {'col'}, dimensions={0}, use_global_device_ids=true | all-gather | bytes 72 | tf_op jit(solution)/shard_map/all_gather | solution.py:46
  38.1 16.3 %all-gather = s32[8,1,1,2]{3,2,1,0:T(1,128)S(1)} all-gather(s32[1,1,1,2]{3,2,1,0:T(1,128)S(1)} %get-tuple-element.11), channel_id=2, replica_groups=mesh['row'=4,'col'=8] {'col'}, dimensions={0}, use_global_device_ids=true | all-gather | bytes 72 | tf_op jit(solution)/shard_map/all_gather | solution.py:46
  54.4 3.3 %all-to-all-start.1 = ((s32[4,1,2]{2,1,0:T(1,128)}), s32[4,1,2]{2,1,0:T(1,128)S(1)}, u32[]{:S(2)}, u32[]{:S(2)}) async-start(s32[4,1,2]{2,1,0:T(1,128)} %copy.119), calls=%async_computation.1 | async-start | bytes 4096 | tf_op jit(solution)/shard_map/all_to_all | solution.py:48
  57.7 3.6 %all-to-all-done.1 = s32[4,1,2]{2,1,0:T(1,128)S(1)} async-done(((s32[4,1,2]{2,1,0:T(1,128)}), s32[4,1,2]{2,1,0:T(1,128)S(1)}, u32[]{:S(2)}, u32[]{:S(2)}) %all-to-all-start.1) | async-done | bytes 64 | tf_op jit(solution)/shard_map/all_to_all | solution.py:48
  61.7 0.1 copy.107
  61.8 0.1 copy.121
  62.3 0.6 gather_fusion.3
  62.9 0.1 copy.142
  63.6 0.6 gather_fusion
  64.2 0.1 copy.140
  64.5 1.8 %gather_fusion.5 = f32[8,128,128]{2,1,0:T(8,128)S(1)} fusion(f32[4,4,128,128]{3,2,1,0:T(8,128)} %bitcast.94, s32[8]{0:T(128)S(1)} %reshape.274), kind=kCustom, calls=%fused_computation.5 | custom fusion | bytes 1048640 | tf_op jit(solution)/shard_map/gather | solution.py:54
  66.4 1.8 %gather_fusion.2 = f32[8,128,128]{2,1,0:T(8,128)S(1)} fusion(f32[4,4,128,128]{3,2,1,0:T(8,128)} %bitcast.95, s32[8]{0:T(128)S(1)} %reshape.252), kind=kCustom, calls=%fused_computation.2 | custom fusion | bytes 1048640 | tf_op jit(solution)/shard_map/gather | solution.py:54
  68.2 20.8 %all-gather.15.cloned.1.call-done = f32[8,1,1,2,128,128]{5,4,3,2,1,0:T(8,128)} async-done(((f32[1,1,1,2,128,128]{5,4,3,2,1,0:T(8,128)}), f32[8,1,1,2,128,128]{5,4,3,2,1,0:T(8,128)}) %all-gather.15.cloned.1.call-update) | async-done | bytes 1048592 | tf_op jit(solution)/shard_map/all_gather | solution.py:45
  89.0 1.8 %gather_fusion.4 = f32[8,2,128,128]{3,2,1,0:T(8,128)S(1)} fusion(f32[8,2,128,128]{3,2,1,0:T(8,128)} %bitcast.90, s32[1024]{0:T(1024)S(1)} %pad_clamp_fusion.1), kind=kCustom, calls=%fused_computation.4 | custom fusion | bytes 2097184 | tf_op jit(solution)/shard_map/gather | solution.py:18
  90.9 39.1 %all-gather.11.cloned.1.call-done = f32[8,1,1,2,128,128]{5,4,3,2,1,0:T(8,128)} async-done(((f32[1,1,1,2,128,128]{5,4,3,2,1,0:T(8,128)}), f32[8,1,1,2,128,128]{5,4,3,2,1,0:T(8,128)}) %all-gather.11.cloned.1.call-update) | async-done | bytes 1048592 | tf_op jit(solution)/shard_map/all_gather | solution.py:45
  129.9 1.8 %gather_fusion.1 = f32[8,2,128,128]{3,2,1,0:T(8,128)S(1)} fusion(f32[8,2,128,128]{3,2,1,0:T(8,128)} %bitcast.91, s32[1024]{0:T(1024)S(1)} %pad_clamp_fusion.2), kind=kCustom, calls=%fused_computation.1 | custom fusion | bytes 2097184 | tf_op jit(solution)/shard_map/gather | solution.py:18
  131.8 1.1 fusion.3
  132.9 1.6 %convolution_bitcast_fusion = f32[8,128,128]{2,0,1:T(8,128)S(1)} fusion(f32[4,2,2,128,128]{4,3,2,1,0:T(8,128)S(1)} %fusion.3, s32[4,2,2]{0,1,2:T(2,128)S(1)} %copy.127), kind=kOutput, calls=%fused_computation.7 | convolution fusion | flops 25165952 | bytes 1572928 | tf_op jit(solution)/shard_map/qtnc,qtnxz->cxz/dot_general | solution.py:29
  134.5 1.1 fusion.5
  135.6 1.6 %fusion = f32[8,128,128]{2,0,1:T(8,128)S(1)} fusion(f32[8,128,128]{2,0,1:T(8,128)S(1)} %convolution_bitcast_fusion, f32[4,2,2,128,128]{4,3,2,1,0:T(8,128)S(1)} %fusion.5, s32[4,2,2]{0,1,2:T(2,128)S(1)} %copy.113), kind=kOutput, calls=%fused_computation.9 | convolution fusion | flops 25297024 | bytes 2097216 | tf_op jit(solution)/shard_map/qtnc,qtnxz->cxz/dot_general | solution.py:29
  137.4 0.6 gather_fusion.6
  137.9 0.4 copy-done
  138.3 0.7 bitcast_add_fusion
  (55 shorter events, 2.0 us)
Async XLA Ops:
  6.5 58.0 %all-gather.17.cloned.1.call-start = ((), (), s32[]{:S(2)}) async-start(), calls=%async_computation.5 | async-start | bytes 1310720 | tf_op jit(solution)/shard_map/all_gather | solution.py:51
  8.4 0.9 copy-start.1
  8.4 57.9 %all-gather.13.cloned.1.call-start = ((), (), s32[]{:S(2)}) async-start(), calls=%async_computation.3 | async-start | bytes 1310720 | tf_op jit(solution)/shard_map/all_gather | solution.py:51
  9.2 79.8 %all-gather.15.cloned.1.call-start = ((), (), s32[]{:S(2)}) async-start(), calls=%async_computation.4 | async-start | bytes 1179648 | tf_op jit(solution)/shard_map/all_gather | solution.py:45
  10.1 0.7 copy-start.2
  11.4 42.9 %all-to-all-start = ((s32[4,1,2]{2,1,0:T(1,128)}), s32[4,1,2]{2,1,0:T(1,128)S(1)}, u32[]{:S(2)}, u32[]{:S(2)}) async-start(s32[4,1,2]{2,1,0:T(1,128)} %copy.105), calls=%async_computation | async-start | bytes 4096 | tf_op jit(solution)/shard_map/all_to_all | solution.py:48
  15.6 114.3 %all-gather.11.cloned.1.call-start = ((), (), s32[]{:S(2)}) async-start(), calls=%async_computation.2 | async-start | bytes 1179648 | tf_op jit(solution)/shard_map/all_gather | solution.py:45
  16.2 0.7 copy-start.3
  38.1 16.3 %copy-start.4 = (s32[1,1,4]{2,1,0:T(1,128)S(1)}, s32[1,1,4]{2,1,0:T(1,128)}, u32[]{:S(2)}) copy-start(s32[1,1,4]{2,1,0:T(1,128)} %param.11) | copy-start | bytes 52
  54.4 7.0 %all-to-all-start.1 = ((s32[4,1,2]{2,1,0:T(1,128)}), s32[4,1,2]{2,1,0:T(1,128)S(1)}, u32[]{:S(2)}, u32[]{:S(2)}) async-start(s32[4,1,2]{2,1,0:T(1,128)} %copy.119), calls=%async_computation.1 | async-start | bytes 4096 | tf_op jit(solution)/shard_map/all_to_all | solution.py:48
  137.3 1.0 copy-start
Sparse Core Ops, SparseCore 0:
  8.9 19.4 all-gather.16
  29.9 16.7 all-gather.12
  48.8 40.1 all-gather.14
  91.0 38.8 all-gather.10
where the time goes:
time: 146 us
  waiting for transfers between devices  64.9 us (44%)
  blocking collectives  37.5 us (26%)
  local copies, waits for them, and re-layouts  16.1 us (11%)
  between operations  13.3 us (9%)
  starting transfers between devices  7.54 us (5%)
  matrix products  5.43 us (4%)
    all_gather x2, waiting for transfers between devices, body(): lax.all_gather(a_blocks[0, :, section_index], 'col', axis=0, tiled=True)  59.9 us
    all_gather x2, blocking collectives, body(): lax.all_gather(a_rows[0, :, section_index], 'col', axis=0, tiled=True)  37.5 us
    all_to_all x2, starting transfers between devices, body(): lax.all_to_all(send_list[0, 0, section_index], 'row', split_axis=0, conca...  7.46 us
    gather x2, local copies, waits for them, and re-layouts, accumulate(): a_chosen = row_panel[inner]  3.67 us
    all_to_all x2, waiting for transfers between devices, body(): lax.all_to_all(send_list[0, 0, section_index], 'row', split_axis=0, conca...  3.64 us
    gather x2, local copies, waits for them, and re-layouts, body(): chosen = shards[picker, jnp.maximum(arrived_lists, 0)]  3.61 us
    dot_general x2, matrix products, accumulate(): jnp.einsum('qtnc,qtnxz->cxz', onehot, products, precision=lax.Precision.H...  3.23 us
  transfers between devices with their start and end apart: 6, of which 3 were waited for; matrix products, arithmetic and copies ran while one was open for 7% of the time, Pallas kernels for 0%

commit v1 on v0

v1 whole, which is shorter than its diff:
```python
import functools

import jax
import jax.numpy as jnp
from jax import lax
from jax.experimental import pallas as pl
from jax.experimental.pallas import tpu as pltpu
from jax.sharding import PartitionSpec as P

BS = 128
SECTIONS = 2
NA = 2
SLOT = 2
NC = 4
NB = 4
CB = 2
BLOCKS = SECTIONS * NA
SLOTS = SECTIONS * SLOT
EARLY = 3
MESH = pl.DeviceIdType.MESH


def kernel(R, N, arows, slist, clist, a_ref, b_ref, cp_ref, out_ref,
           abuf, bsrc, stage, bbuf, bhi, blo, mtile, mbuf, msm,
           zsend, zrecv, ysend, yrecv, bsend, brecv, msend, mrecv, lsem):
    L = N // 2
    row = lax.axis_index("row")
    col = lax.axis_index("col")
    z = col // 2
    y = col % 2
    pair = 2 * z + 1 - y

    b_in = pltpu.make_async_copy(b_ref.at[0, 0], bsrc, lsem.at[0])
    a_in = pltpu.make_async_copy(a_ref.at[0, 0], abuf.at[col], lsem.at[1])
    c_in = pltpu.make_async_copy(cp_ref.at[0, 0], out_ref.at[0, 0], lsem.at[2])
    b_in.start()
    a_in.start()
    c_in.start()

    barrier = pltpu.get_barrier_semaphore()
    for o in range(1, N):
        pl.semaphore_signal(barrier, inc=1, device_id=(row, (col + o) % N), device_id_type=MESH)
    for o in range(1, R):
        pl.semaphore_signal(barrier, inc=1, device_id=((row + o) % R, col), device_id_type=MESH)

    lane = lax.broadcasted_iota(jnp.int32, (1, 128), 1)
    tile = jnp.zeros((1, 128), jnp.int32)
    for s in range(SECTIONS):
        for a in range(NA):
            tile = jnp.where(lane == s * NA + a, arows[0, 0, s, a], tile)
        for r in range(R):
            for t in range(SLOT):
                tile = jnp.where(lane == BLOCKS + (s * R + r) * SLOT + t, slist[0, 0, s, r, t], tile)
    mtile[...] = tile
    mbuf[col] = tile
    mbuf[N + row] = tile
    bbuf[R * SLOTS] = jnp.zeros((BS, BS), jnp.float32)

    pl.semaphore_wait(barrier, N - 1 + R - 1)

    def own(k):
        return a_ref.at[0, 0, k // NA, k % NA]

    def held(src, k):
        return abuf.at[src, k // NA, k % NA]

    def line(up, d, ci, first=False):
        begin = z - (d - 1) if up else z + (d - 1)
        src = 2 * begin + (y if ci < BLOCKS else 1 - y)
        k = ci if ci < BLOCKS else EARLY
        way = 0 if up else 1
        return pltpu.make_async_remote_copy(
            src_ref=own(k) if first and ci < BLOCKS else held(src, k),
            dst_ref=held(src, k),
            send_sem=zsend.at[way, d - 1, ci],
            recv_sem=zrecv.at[way, d - 1, ci],
            device_id=(row, col + 2 if up else col - 2),
            device_id_type=MESH,
        )

    def line_sends(up, d):
        return jnp.logical_and(z + 1 < L, z - (d - 1) >= 0) if up else jnp.logical_and(z >= 1, z + (d - 1) < L)

    def line_gets(up, d):
        return z - d >= 0 if up else z + d < L

    def line_got(up, d, ci):
        begin = z - d if up else z + d
        src = 2 * begin + (y if ci < BLOCKS else 1 - y)
        k = ci if ci < BLOCKS else EARLY
        way = 0 if up else 1
        return pltpu.make_async_remote_copy(
            src_ref=held(src, k), dst_ref=held(src, k),
            send_sem=zsend.at[way, d - 1, ci], recv_sem=zrecv.at[way, d - 1, ci],
            device_id=(row, pair), device_id_type=MESH)

    def across(begin, k, first=False):
        src = 2 * begin + y
        return pltpu.make_async_remote_copy(
            src_ref=own(k) if first else held(src, k), dst_ref=held(src, k),
            send_sem=ysend.at[begin, k], recv_sem=yrecv.at[begin, k],
            device_id=(row, pair), device_id_type=MESH)

    def across_got(begin, k):
        src = 2 * begin + 1 - y
        return pltpu.make_async_remote_copy(
            src_ref=held(src, k), dst_ref=held(src, k),
            send_sem=ysend.at[begin, k], recv_sem=yrecv.at[begin, k],
            device_id=(row, pair), device_id_type=MESH)

    order = (EARLY,) + tuple(k for k in range(BLOCKS) if k != EARLY)
    late = tuple(k for k in range(BLOCKS) if k != EARLY)
    for k in order:
        across(z, k, True).start()
        for up in (True, False):
            pl.when(line_sends(up, 1))(lambda up=up, k=k: line(up, 1, k, True).start())

    def tell(o, along_col):
        at = o if along_col else N + o
        to = (row, (col + o) % N) if along_col else ((row + o) % R, col)
        place = col if along_col else N + row
        return pltpu.make_async_remote_copy(
            src_ref=mtile, dst_ref=mbuf.at[place], send_sem=msend.at[at], recv_sem=mrecv.at[at],
            device_id=to, device_id_type=MESH)

    def told(o, along_col):
        at = o if along_col else N + o
        place = (col - o + N) % N if along_col else N + (row - o + R) % R
        return pltpu.make_async_remote_copy(
            src_ref=mtile, dst_ref=mbuf.at[place], send_sem=msend.at[at], recv_sem=mrecv.at[at],
            device_id=(row, pair), device_id_type=MESH)

    peers = [(o, True) for o in range(1, N)] + [(o, False) for o in range(1, R)]
    for peer in peers:
        tell(*peer).start()

    b_in.wait()

    def give(o):
        return pltpu.make_async_remote_copy(
            src_ref=stage.at[o], dst_ref=bbuf.at[pl.ds(row * SLOTS, SLOTS)],
            send_sem=bsend.at[o], recv_sem=brecv.at[o],
            device_id=((row + o) % R, col), device_id_type=MESH)

    def given(o):
        q = (row - o + R) % R
        return pltpu.make_async_remote_copy(
            src_ref=stage.at[o], dst_ref=bbuf.at[pl.ds(q * SLOTS, SLOTS)],
            send_sem=bsend.at[o], recv_sem=brecv.at[o],
            device_id=((row + o) % R, col), device_id_type=MESH)

    for o in sorted(range(R), key=lambda o: (o == 0, abs(o - R // 2))):
        to = (row + o) % R
        for s in range(SECTIONS):
            for t in range(SLOT):
                entry = jnp.maximum(slist[0, 0, s, to, t], 0)
                if o:
                    stage[o, s * SLOT + t] = bsrc[s, entry]
                else:
                    bbuf[row * SLOTS + s * SLOT + t] = bsrc[s, entry]
        if o:
            give(o).start()

    across_got(z, EARLY).wait_recv()
    for up in (True, False):
        pl.when(line_sends(up, 1))(lambda up=up: line(up, 1, BLOCKS).start())

    def step(d, carry):
        for ci in late + (EARLY, BLOCKS):
            for up in (True, False):
                @pl.when(line_gets(up, d))
                def _():
                    line_got(up, d, ci).wait_recv()
                    pl.when(line_sends(up, d + 1))(lambda: line(up, d + 1, ci).start())
                    if ci in late:
                        across(z - d if up else z + d, ci).start()
        return carry

    lax.fori_loop(1, L, step, 0)

    a_in.wait()
    c_in.wait()
    for peer in peers:
        told(*peer).wait_recv()
    to_scalar = pltpu.make_async_copy(mbuf, msm, lsem.at[3])
    to_scalar.start()
    for o in range(1, R):
        given(o).wait_recv()

    def split(at, carry):
        block = bbuf[at]
        high = block.astype(jnp.bfloat16)
        bhi[at] = high
        blo[at] = (block - high.astype(jnp.float32)).astype(jnp.bfloat16)
        return carry

    lax.fori_loop(0, R * SLOTS + 1, split, 0)
    to_scalar.wait()

    for begin in range(L):
        for k in late:
            across_got(begin, k).wait_recv()

    none = R * SLOTS
    wanted_i = [clist[0, 0, m] // CB for m in range(NC)]
    wanted_j = [clist[0, 0, m] % CB for m in range(NC)]

    def multiply(src):
        q = src // 2
        h = src % 2
        for s in range(SECTIONS):
            first = q * SLOTS + s * SLOT
            filled = [msm[N + q, 0, BLOCKS + (s * R + row) * SLOT + t] for t in range(SLOT)]
            at = []
            for j in range(CB):
                entry = h * CB + j
                at.append(jnp.where(filled[0] == entry, first, jnp.where(filled[1] == entry, first + 1, none)))
            rows = [msm[src, 0, s * NA + a] for a in range(NA)]
            left = jnp.concatenate([abuf[src, s, a] for a in range(NA)], axis=1)
            lhi = left.astype(jnp.bfloat16)
            llo = (left - lhi.astype(jnp.float32)).astype(jnp.bfloat16)
            highs, lows = [], []
            for m in range(NC):
                slot = jnp.where(wanted_j[m] == 0, at[0], at[1])
                places = [jnp.where(rows[a] == wanted_i[m], slot, none) for a in range(NA)]
                highs.append(jnp.concatenate([bhi[p] for p in places], axis=0))
                lows.append(jnp.concatenate([blo[p] for p in places], axis=0))
            rhi = jnp.concatenate(highs, axis=1)
            rlo = jnp.concatenate(lows, axis=1)
            total = jnp.dot(lhi, rhi, preferred_element_type=jnp.float32)
            total += jnp.dot(lhi, rlo, preferred_element_type=jnp.float32)
            total += jnp.dot(llo, rhi, preferred_element_type=jnp.float32)
            for m in range(NC):
                out_ref[0, 0, m] += total[:, m * BS:(m + 1) * BS]

    def all_of(src, carry):
        multiply(src)
        return carry

    lax.fori_loop(0, N, all_of, 0)

    for begin in range(L):
        for k in late:
            across(begin, k).wait_send()
    across(z, EARLY).wait_send()

    def drain(d, carry):
        for ci in range(BLOCKS + 1):
            for up in (True, False):
                pl.when(line_sends(up, d))(lambda up=up, ci=ci: line(up, d, ci).wait_send())
        return carry

    lax.fori_loop(1, L, drain, 0)
    for o in range(1, R):
        give(o).wait_send()
    for peer in peers:
        tell(*peer).wait_send()


def body(a_blocks, a_rows, b_blocks, send_list, c_partial, c_list):
    R = lax.axis_size("row")
    N = lax.axis_size("col")
    L = N // 2
    smem = pl.BlockSpec(memory_space=pltpu.SMEM)
    hbm = pl.BlockSpec(memory_space=pl.ANY)
    dma = pltpu.SemaphoreType.DMA
    return pl.pallas_call(
        functools.partial(kernel, R, N),
        out_shape=jax.ShapeDtypeStruct((1, 1, NC, BS, BS), jnp.float32),
        in_specs=[smem, smem, smem, hbm, hbm, hbm],
        out_specs=pl.BlockSpec(memory_space=pltpu.VMEM),
        scratch_shapes=[
            pltpu.VMEM((N, SECTIONS, NA, BS, BS), jnp.float32),
            pltpu.VMEM((SECTIONS, NB, BS, BS), jnp.float32),
            pltpu.VMEM((R, SLOTS, BS, BS), jnp.float32),
            pltpu.VMEM((R * SLOTS + 1, BS, BS), jnp.float32),
            pltpu.VMEM((R * SLOTS + 1, BS, BS), jnp.bfloat16),
            pltpu.VMEM((R * SLOTS + 1, BS, BS), jnp.bfloat16),
            pltpu.VMEM((1, 128), jnp.int32),
            pltpu.VMEM((N + R, 1, 128), jnp.int32),
            pltpu.SMEM((N + R, 1, 128), jnp.int32),
            dma((2, L, BLOCKS + 1)),
            dma((2, L, BLOCKS + 1)),
            dma((L, BLOCKS)),
            dma((L, BLOCKS)),
            dma((R,)),
            dma((R,)),
            dma((N + R,)),
            dma((N + R,)),
            dma((4,)),
        ],
        compiler_params=pltpu.CompilerParams(
            collective_id=0, has_side_effects=True, vmem_limit_bytes=48 * 1024 * 1024
        ),
    )(a_rows, send_list, c_list, a_blocks, b_blocks, c_partial)


def solution(mesh):
    placed = (
        P("row", "col", None, None, None, None),
        P("row", "col", None, None),
        P("row", "col", None, None, None, None),
        P("row", "col", None, None, None),
        P("row", "col", None, None, None),
        P("row", "col", None),
    )
    return jax.shard_map(
        body,
        mesh=mesh,
        in_specs=placed,
        out_specs=P("row", "col", None, None, None),
        check_vma=False,
    )
```

time: 146 us -> 39.3 us (0.27)
  waiting for transfers between devices: 64.9 us -> 0 us
  blocking collectives: 37.5 us -> 0 us
  Pallas kernels: 0 us -> 34.6 us
  between operations: 13.3 us -> 0.01 us
  local copies, waits for them, and re-layouts: 16.1 us -> 4.45 us
  starting transfers between devices: 7.54 us -> 0 us
  matrix products: 5.43 us -> 0 us
    all_gather x4 -> x0, waiting for transfers between devices: 59.9 us -> none  [the longest x2 59.9 us: body(): lax.all_gather(a_blocks[0, :, section_index], 'col', axis=0, tiled=True)]
    all_gather x2 -> x0, blocking collectives: 37.5 us -> none  [body(): lax.all_gather(a_rows[0, :, section_index], 'col', axis=0, tiled=True)]
    pallas_call x0 -> x1, Pallas kernels: none -> 34.6 us  [body(): pl.pallas_call(functools.partial(kernel, R, N), out_shape=jax.ShapeDtypeS...]
    gather x7 -> x0, local copies, waits for them, and re-layouts: 8.97 us -> none  [the longest x2 3.67 us: accumulate(): a_chosen = row_panel[inner]]
    all_to_all x2 -> x0, starting transfers between devices: 7.46 us -> none  [body(): lax.all_to_all(send_list[0, 0, section_index], 'row', split_axis=0, conca...]
    dot_general x4 -> x0, matrix products: 5.43 us -> none  [the longest x2 3.23 us: accumulate(): jnp.einsum('qtnc,qtnxz->cxz', onehot, products, precision=lax.Precision.H...]
    all_to_all x2 -> x0, waiting for transfers between devices: 3.64 us -> none  [body(): lax.all_to_all(send_list[0, 0, section_index], 'row', split_axis=0, conca...]
    unnamed x12, local copies, waits for them, and re-layouts: 1.18 us -> 4.45 us
  transfers between devices with their start and end apart: 6 -> 0, of which waited for: 3 -> 0; matrix products, arithmetic and copies ran while one was open for 7% -> 0% of each run, Pallas kernels for 0% -> 0%
where the time goes in v1:
time: 39.3 us; the launch traced here: 39 us
  Pallas kernels  34.6 us (88%)
  local copies, waits for them, and re-layouts  4.45 us (11%)
    pallas_call x1, Pallas kernels, body(): pl.pallas_call(functools.partial(kernel, R, N), out_shape=jax.ShapeDtypeS...  34.6 us
    unnamed x12, local copies, waits for them, and re-layouts  4.45 us

profile of v1, /device:TPU:0, one launch (start us, length us, event | category | flops | bytes accessed | tf_op | source)
XLA Modules:
  0.0 39.0 jit_solution(8254838225129636489)
XLA Ops:
  0.0 0.0 copy-start.4
  0.0 0.0 copy-start.3
  0.0 0.8 %copy.7.slist = s32[1,1,2,4,2]{4,3,2,1,0:T(4,128)S(1)} copy(s32[1,1,2,4,2]{3,4,2,1,0:T(2,128)} %param.9) | data formatting | bytes 128 | tf_op args[3]
  0.8 0.0 copy-done.4
  0.8 0.0 copy-done.3
  0.8 0.0 copy-start
  0.8 1.0 %copy-done = f32[1,1,2,4,128,128]{5,4,3,2,1,0:T(8,128)S(1)} copy-done((f32[1,1,2,4,128,128]{5,4,3,2,1,0:T(8,128)S(1)}, f32[1,1,2,4,128,128]{5,4,3,2,1,0:T(8,128)}, u32[]{:S(2)}) %copy-start) | copy-done | bytes 524312
  1.9 0.0 copy-start.1
  1.9 0.9 %copy-done.1 = f32[1,1,2,2,128,128]{5,4,3,2,1,0:T(8,128)S(1)} copy-done((f32[1,1,2,2,128,128]{5,4,3,2,1,0:T(8,128)S(1)}, f32[1,1,2,2,128,128]{5,4,3,2,1,0:T(8,128)}, u32[]{:S(2)}) %copy-start.1) | copy-done | bytes 262168
  2.8 0.0 copy-start.2
  2.8 0.9 %copy-done.2 = f32[1,1,4,128,128]{4,3,2,1,0:T(8,128)S(1)} copy-done((f32[1,1,4,128,128]{4,3,2,1,0:T(8,128)S(1)}, f32[1,1,4,128,128]{4,3,2,1,0:T(8,128)}, u32[]{:S(2)}) %copy-start.2) | copy-done | bytes 262168
  3.8 34.6 %shard_map.64 = f32[1,1,4,128,128]{4,3,2,1,0:T(8,128)S(1)} custom-call(s32[1,1,2,2]{3,2,1,0:T(2,128)S(1)} %copy-done.3, s32[1,1,2,4,2]{4,3,2,1,0:T(4,128)S(1)} %copy.7.slist, s32[1,1,4]{2,1,0:T(1,128)S(1)} %copy-done.4, f32[1,1,2,2,128,128]{5,4,3,2,1,0:T(8,128)S(1)} %copy-done.1, f32[1,1,2,4,128,128]{5,4,3,2,1,0:T(8,128)S(1)} %copy-done, ...), custom_call_target="tpu_custom_call" | custom-call | tf_op jit(solution)/shard_map/pallas_call | solution.py:267
  38.3 0.7 %copy.9 = f32[1,1,4,128,128]{4,3,2,1,0:T(8,128)} copy(f32[1,1,4,128,128]{4,3,2,1,0:T(8,128)S(1)} %shard_map.64) | data formatting | bytes 524288
Async XLA Ops:
  0.0 0.8 %copy-start.4 = (s32[1,1,4]{2,1,0:T(1,128)S(1)}, s32[1,1,4]{2,1,0:T(1,128)}, u32[]{:S(2)}) copy-start(s32[1,1,4]{2,1,0:T(1,128)} %clist.1) | copy-start | bytes 52
  0.0 0.8 %copy-start.3 = (s32[1,1,2,2]{3,2,1,0:T(2,128)S(1)}, s32[1,1,2,2]{3,2,1,0:T(2,128)}, u32[]{:S(2)}) copy-start(s32[1,1,2,2]{3,2,1,0:T(2,128)} %arows.1) | copy-start | bytes 52
  0.8 1.0 %copy-start = (f32[1,1,2,4,128,128]{5,4,3,2,1,0:T(8,128)S(1)}, f32[1,1,2,4,128,128]{5,4,3,2,1,0:T(8,128)}, u32[]{:S(2)}) copy-start(f32[1,1,2,4,128,128]{5,4,3,2,1,0:T(8,128)} %b_ref.1) | copy-start | bytes 1572868
  1.9 0.9 %copy-start.1 = (f32[1,1,2,2,128,128]{5,4,3,2,1,0:T(8,128)S(1)}, f32[1,1,2,2,128,128]{5,4,3,2,1,0:T(8,128)}, u32[]{:S(2)}) copy-start(f32[1,1,2,2,128,128]{5,4,3,2,1,0:T(8,128)} %a_ref.1) | copy-start | bytes 786436
  2.8 0.9 %copy-start.2 = (f32[1,1,4,128,128]{4,3,2,1,0:T(8,128)S(1)}, f32[1,1,4,128,128]{4,3,2,1,0:T(8,128)}, u32[]{:S(2)}) copy-start(f32[1,1,4,128,128]{4,3,2,1,0:T(8,128)} %cp_ref.1) | copy-start | bytes 786436

commit v2 on v1

v2 whole, which is shorter than its diff:
```python
import functools

import jax
import jax.numpy as jnp
from jax import lax
from jax.experimental import pallas as pl
from jax.experimental.pallas import tpu as pltpu
from jax.sharding import PartitionSpec as P

BS = 128
SECTIONS = 2
NA = 2
SLOT = 2
NC = 4
NB = 4
CB = 2
BLOCKS = SECTIONS * NA
SLOTS = SECTIONS * SLOT
ROWS = BLOCKS * BS
CUTS = (0, 88, 192, 296, 400, ROWS)
PIECES = len(CUTS) - 1
EARLY = 0
LISTS = PIECES
LATE = (LISTS,) + tuple(range(1, PIECES))
OTHER = PIECES + 1
LINE = (LISTS, EARLY) + tuple(range(1, PIECES)) + (OTHER,)
MESH = pl.DeviceIdType.MESH


def kernel(R, N, arows, slist, clist, a_ref, b_ref, cp_ref, out_ref,
           abuf, bsrc, stage, bbuf, bhi, blo, mtile, mbuf, msm,
           zsend, zrecv, ysend, yrecv, bsend, brecv, msend, mrecv, msem, lsem):
    L = N // 2
    row = lax.axis_index("row")
    col = lax.axis_index("col")
    z = col // 2
    y = col % 2
    pair = 2 * z + 1 - y

    barrier = pltpu.get_barrier_semaphore()
    pl.when(z + 1 < L)(lambda: pl.semaphore_signal(barrier, inc=1, device_id=(row, col + 2), device_id_type=MESH))
    pl.when(z >= 1)(lambda: pl.semaphore_signal(barrier, inc=1, device_id=(row, col - 2), device_id_type=MESH))
    pl.semaphore_signal(barrier, inc=1, device_id=(row, pair), device_id_type=MESH)
    for o in range(1, R):
        pl.semaphore_signal(barrier, inc=1, device_id=((row + o) % R, col), device_id_type=MESH)

    b_in = pltpu.make_async_copy(b_ref.at[0, 0], bsrc, lsem.at[0])
    a_in = pltpu.make_async_copy(a_ref.at[0, 0], abuf.at[col], lsem.at[1])
    c_in = pltpu.make_async_copy(cp_ref.at[0, 0], out_ref.at[0, 0], lsem.at[2])
    b_in.start()
    a_in.start()
    c_in.start()

    lane = lax.broadcasted_iota(jnp.int32, (1, 128), 1)
    tile = jnp.zeros((1, 128), jnp.int32)
    for s in range(SECTIONS):
        for a in range(NA):
            tile = jnp.where(lane == s * NA + a, arows[0, 0, s, a], tile)
        for r in range(R):
            for t in range(SLOT):
                tile = jnp.where(lane == BLOCKS + (s * R + r) * SLOT + t, slist[0, 0, s, t, r], tile)
    mtile[...] = tile
    mbuf[col] = tile
    mbuf[N + row] = tile

    edge = jnp.where(z + 1 < L, 1, 0) + jnp.where(z >= 1, 1, 0)
    pl.semaphore_wait(barrier, R + edge)

    def own(k):
        return mtile if k == LISTS else a_ref.at[0, 0, pl.ds(CUTS[k], CUTS[k + 1] - CUTS[k])]

    def held(src, k):
        return mbuf.at[src] if k == LISTS else abuf.at[src, pl.ds(CUTS[k], CUTS[k + 1] - CUTS[k])]

    def line_piece(begin, ci):
        return (2 * begin + 1 - y, EARLY) if ci == OTHER else (2 * begin + y, ci)

    def line(up, d, ci, first=False):
        src, k = line_piece(z - (d - 1) if up else z + (d - 1), ci)
        way = 0 if up else 1
        return pltpu.make_async_remote_copy(
            src_ref=own(k) if first and ci != OTHER else held(src, k),
            dst_ref=held(src, k),
            send_sem=zsend.at[way, d - 1, ci],
            recv_sem=zrecv.at[way, d - 1, ci],
            device_id=(row, col + 2 if up else col - 2),
            device_id_type=MESH,
        )

    def line_sends(up, d):
        return jnp.logical_and(z + 1 < L, z - (d - 1) >= 0) if up else jnp.logical_and(z >= 1, z + (d - 1) < L)

    def line_gets(up, d):
        return z - d >= 0 if up else z + d < L

    def line_got(up, d, ci):
        src, k = line_piece(z - d if up else z + d, ci)
        way = 0 if up else 1
        return pltpu.make_async_remote_copy(
            src_ref=held(src, k), dst_ref=held(src, k),
            send_sem=zsend.at[way, d - 1, ci], recv_sem=zrecv.at[way, d - 1, ci],
            device_id=(row, pair), device_id_type=MESH)

    def across(begin, k, first=False):
        src = 2 * begin + y
        return pltpu.make_async_remote_copy(
            src_ref=own(k) if first else held(src, k), dst_ref=held(src, k),
            send_sem=ysend.at[begin, k], recv_sem=yrecv.at[begin, k],
            device_id=(row, pair), device_id_type=MESH)

    def across_got(begin, k):
        src = 2 * begin + 1 - y
        return pltpu.make_async_remote_copy(
            src_ref=held(src, k), dst_ref=held(src, k),
            send_sem=ysend.at[begin, k], recv_sem=yrecv.at[begin, k],
            device_id=(row, pair), device_id_type=MESH)

    for k in LINE:
        if k != OTHER:
            across(z, k, True).start()
            for up in (True, False):
                pl.when(line_sends(up, 1))(lambda up=up, k=k: line(up, 1, k, True).start())

    def tell(o):
        return pltpu.make_async_remote_copy(
            src_ref=mtile, dst_ref=mbuf.at[N + row], send_sem=msend.at[o], recv_sem=mrecv.at[o],
            device_id=((row + o) % R, col), device_id_type=MESH)

    def told(o):
        return pltpu.make_async_remote_copy(
            src_ref=mtile, dst_ref=mbuf.at[N + (row - o + R) % R], send_sem=msend.at[o], recv_sem=mrecv.at[o],
            device_id=(row, pair), device_id_type=MESH)

    for o in range(1, R):
        tell(o).start()

    b_in.wait()

    def give(o, q):
        return pltpu.make_async_remote_copy(
            src_ref=stage.at[o], dst_ref=bbuf.at[pl.ds(q * SLOTS, SLOTS)],
            send_sem=bsend.at[o], recv_sem=brecv.at[o],
            device_id=((row + o) % R, col), device_id_type=MESH)

    for o in sorted(range(R), key=lambda o: (o == 0, abs(o - R // 2))):
        to = (row + o) % R
        for s in range(SECTIONS):
            for t in range(SLOT):
                entry = jnp.maximum(slist[0, 0, s, t, to], 0)
                if o:
                    stage[o, s * SLOT + t] = bsrc[s, entry]
                else:
                    bbuf[row * SLOTS + s * SLOT + t] = bsrc[s, entry]
        if o:
            give(o, row).start()

    across_got(z, EARLY).wait_recv()
    for up in (True, False):
        pl.when(line_sends(up, 1))(lambda up=up: line(up, 1, OTHER).start())

    def step(d, carry):
        for ci in LINE:
            for up in (True, False):
                @pl.when(line_gets(up, d))
                def _():
                    line_got(up, d, ci).wait_recv()
                    pl.when(line_sends(up, d + 1))(lambda: line(up, d + 1, ci).start())
                    if ci in LATE:
                        across(z - d if up else z + d, ci).start()
        return carry

    none = R * SLOTS

    def split(at, carry):
        block = bbuf[at]
        high = block.astype(jnp.bfloat16)
        bhi[at] = high
        blo[at] = (block - high.astype(jnp.float32)).astype(jnp.bfloat16)
        return carry

    def lists_in(src):
        return pltpu.make_async_copy(mbuf.at[src], msm.at[src], msem.at[src])

    def each(least, most, do):
        def one(begin, carry):
            away = jnp.maximum(begin - z, z - begin)
            pl.when(jnp.logical_and(away >= least, away <= most))(lambda: do(begin))
            return carry
        lax.fori_loop(0, L, one, 0)

    def lists_across(begin):
        across_got(begin, LISTS).wait_recv()
        lists_in(2 * begin + 1 - y).start()

    wanted_i = [clist[0, 0, m] // CB for m in range(NC)]
    wanted_j = [clist[0, 0, m] % CB for m in range(NC)]

    def multiply(src):
        lists_in(src).wait()
        q = src // 2
        h = src % 2
        for s in range(SECTIONS):
            first = q * SLOTS + s * SLOT
            filled = [msm[N + q, 0, BLOCKS + (s * R + row) * SLOT + t] for t in range(SLOT)]
            at = []
            for j in range(CB):
                entry = h * CB + j
                at.append(jnp.where(filled[0] == entry, first, jnp.where(filled[1] == entry, first + 1, none)))
            rows = [msm[src, 0, s * NA + a] for a in range(NA)]
            left = jnp.concatenate([abuf[src, pl.ds((s * NA + a) * BS, BS)] for a in range(NA)], axis=1)
            lhi = left.astype(jnp.bfloat16)
            llo = (left - lhi.astype(jnp.float32)).astype(jnp.bfloat16)
            highs, lows = [], []
            for m in range(NC):
                slot = jnp.where(wanted_j[m] == 0, at[0], at[1])
                places = [jnp.where(rows[a] == wanted_i[m], slot, none) for a in range(NA)]
                highs.append(jnp.concatenate([bhi[p] for p in places], axis=0))
                lows.append(jnp.concatenate([blo[p] for p in places], axis=0))
            rhi = jnp.concatenate(highs, axis=1)
            rlo = jnp.concatenate(lows, axis=1)
            total = jnp.dot(lhi, rhi, preferred_element_type=jnp.float32)
            total += jnp.dot(lhi, rlo, preferred_element_type=jnp.float32)
            total += jnp.dot(llo, rhi, preferred_element_type=jnp.float32)
            for m in range(NC):
                out_ref[0, 0, m] += total[:, m * BS:(m + 1) * BS]

    def mine(begin):
        multiply(2 * begin + y)

    def theirs(begin):
        for k in LATE[1:]:
            across_got(begin, k).wait_recv()
        multiply(2 * begin + 1 - y)

    near = min(2, L - 1)
    lax.fori_loop(1, near + 1, step, 0)
    each(0, near, lambda begin: lists_in(2 * begin + y).start())
    each(0, 0, lists_across)
    bbuf[none] = jnp.zeros((BS, BS), jnp.float32)
    for o in range(1, R):
        told(o).wait_recv()
    sides = pltpu.make_async_copy(mbuf.at[pl.ds(N, R)], msm.at[pl.ds(N, R)], lsem.at[3])
    sides.start()
    for o in range(1, R):
        give(o, (row - o + R) % R).wait_recv()
    lax.fori_loop(0, none + 1, split, 0)
    sides.wait()
    a_in.wait()
    c_in.wait()
    each(0, near, mine)
    each(0, 0, theirs)
    lax.fori_loop(near + 1, L, step, 0)
    each(near + 1, L - 1, lambda begin: lists_in(2 * begin + y).start())
    each(1, L - 1, lists_across)
    each(1, 1, theirs)
    each(near + 1, L - 1, mine)
    for d in range(2, near + 1):
        each(d, d, theirs)
    each(near + 1, L - 1, theirs)

    for begin in range(L):
        for k in LATE:
            across(begin, k).wait_send()
    across(z, EARLY).wait_send()

    def drain(d, carry):
        for ci in LINE:
            for up in (True, False):
                pl.when(line_sends(up, d))(lambda up=up, ci=ci: line(up, d, ci).wait_send())
        return carry

    lax.fori_loop(1, L, drain, 0)
    for o in range(1, R):
        give(o, row).wait_send()
        tell(o).wait_send()


def body(a_blocks, a_rows, b_blocks, send_list, c_partial, c_list):
    R = lax.axis_size("row")
    N = lax.axis_size("col")
    L = N // 2
    smem = pl.BlockSpec(memory_space=pltpu.SMEM)
    hbm = pl.BlockSpec(memory_space=pl.ANY)
    dma = pltpu.SemaphoreType.DMA
    return pl.pallas_call(
        functools.partial(kernel, R, N),
        out_shape=jax.ShapeDtypeStruct((1, 1, NC, BS, BS), jnp.float32),
        in_specs=[smem, smem, smem, hbm, hbm, hbm],
        out_specs=pl.BlockSpec(memory_space=pltpu.VMEM),
        scratch_shapes=[
            pltpu.VMEM((N, ROWS, BS), jnp.float32),
            pltpu.VMEM((SECTIONS, NB, BS, BS), jnp.float32),
            pltpu.VMEM((R, SLOTS, BS, BS), jnp.float32),
            pltpu.VMEM((R * SLOTS + 1, BS, BS), jnp.float32),
            pltpu.VMEM((R * SLOTS + 1, BS, BS), jnp.bfloat16),
            pltpu.VMEM((R * SLOTS + 1, BS, BS), jnp.bfloat16),
            pltpu.VMEM((1, 128), jnp.int32),
            pltpu.VMEM((N + R, 1, 128), jnp.int32),
            pltpu.SMEM((N + R, 1, 128), jnp.int32),
            dma((2, L, PIECES + 2)),
            dma((2, L, PIECES + 2)),
            dma((L, PIECES + 1)),
            dma((L, PIECES + 1)),
            dma((R,)),
            dma((R,)),
            dma((R,)),
            dma((R,)),
            dma((N,)),
            dma((4,)),
        ],
        compiler_params=pltpu.CompilerParams(
            collective_id=0, has_side_effects=True, vmem_limit_bytes=62 * 1024 * 1024
        ),
    )(
        a_rows, jnp.swapaxes(send_list, 3, 4), c_list,
        a_blocks.reshape(1, 1, ROWS, BS), b_blocks, c_partial,
    )


def solution(mesh):
    placed = (
        P("row", "col", None, None, None, None),
        P("row", "col", None, None),
        P("row", "col", None, None, None, None),
        P("row", "col", None, None, None),
        P("row", "col", None, None, None),
        P("row", "col", None),
    )
    return jax.shard_map(
        body,
        mesh=mesh,
        in_specs=placed,
        out_specs=P("row", "col", None, None, None),
        check_vma=False,
    )
```

time: 39.3 us -> 34.3 us (0.87)
  local copies, waits for them, and re-layouts: 4.45 us -> 1.67 us
  Pallas kernels: 34.6 us -> 32.4 us
    unnamed x12 -> x1, local copies, waits for them, and re-layouts: 4.45 us -> 1.67 us
    pallas_call x1, Pallas kernels: 34.6 us -> 32.4 us  [body(): pl.pallas_call(functools.partial(kernel, R, N), out_shape=jax.ShapeDtypeS...]
where the time goes in v2:
time: 34.3 us; the launch traced here: 34.1 us
  Pallas kernels  32.4 us (94%)
  local copies, waits for them, and re-layouts  1.67 us (5%)
    pallas_call x1, Pallas kernels, body(): pl.pallas_call(functools.partial(kernel, R, N), out_shape=jax.ShapeDtypeS...  32.4 us
    unnamed x1, local copies, waits for them, and re-layouts  1.67 us

profile of v2, /device:TPU:0, one launch (start us, length us, event | category | flops | bytes accessed | tf_op | source)
XLA Modules:
  0.0 34.1 jit_solution(11105863135247844074)
XLA Ops:
  0.0 32.4 %shard_map.64 = f32[1,1,4,128,128]{4,3,2,1,0:T(8,128)} custom-call(s32[1,1,2,2]{3,2,1,0:T(2,128)} %arows.1, s32[1,1,2,2,4]{4,3,2,1,0:T(2,128)} %bitcast.3, s32[1,1,4]{2,1,0:T(1,128)} %clist.1, f32[1,1,512,128]{3,2,1,0:T(8,128)} %bitcast.2, f32[1,1,2,4,128,128]{5,4,3,2,1,0:T(8,128)} %b_ref.1, f32[1,1,4,128,128]{4,3,2,1,0:T(8,128)} %cp_ref.1), custom_call_target="tpu_custom_call" | custom-call | tf_op jit(solution)/shard_map/pallas_call | solution.py:285
  32.5 1.7 %copy.8 = f32[1,1,4,128,128]{4,3,2,1,0:T(8,128)} copy(f32[1,1,4,128,128]{4,3,2,1,0:T(8,128)} %shard_map.64) | data formatting | bytes 524288

commit v3 on v2

--- a/solution.py
+++ b/solution.py
@@ -17,13 +17,13 @@
 BLOCKS = SECTIONS * NA
 SLOTS = SECTIONS * SLOT
 ROWS = BLOCKS * BS
-CUTS = (0, 88, 192, 296, 400, ROWS)
+CUTS = (0, 64, 128, 320, ROWS)
 PIECES = len(CUTS) - 1
-EARLY = 0
 LISTS = PIECES
-LATE = (LISTS,) + tuple(range(1, PIECES))
-OTHER = PIECES + 1
-LINE = (LISTS, EARLY) + tuple(range(1, PIECES)) + (OTHER,)
+EARLY = (0, 1)
+LATE = (LISTS,) + tuple(k for k in range(PIECES) if k not in EARLY)
+OTHER = tuple(PIECES + 1 + k for k in range(len(EARLY)))
+LINE = LATE + EARLY + OTHER
 MESH = pl.DeviceIdType.MESH
 
 
@@ -73,13 +73,13 @@
         return mbuf.at[src] if k == LISTS else abuf.at[src, pl.ds(CUTS[k], CUTS[k + 1] - CUTS[k])]
 
     def line_piece(begin, ci):
-        return (2 * begin + 1 - y, EARLY) if ci == OTHER else (2 * begin + y, ci)
+        return (2 * begin + 1 - y, EARLY[ci - PIECES - 1]) if ci in OTHER else (2 * begin + y, ci)
 
     def line(up, d, ci, first=False):
         src, k = line_piece(z - (d - 1) if up else z + (d - 1), ci)
         way = 0 if up else 1
         return pltpu.make_async_remote_copy(
-            src_ref=own(k) if first and ci != OTHER else held(src, k),
+            src_ref=own(k) if first and ci not in OTHER else held(src, k),
             dst_ref=held(src, k),
             send_sem=zsend.at[way, d - 1, ci],
             recv_sem=zrecv.at[way, d - 1, ci],
@@ -87,11 +87,21 @@
             device_id_type=MESH,
         )
 
-    def line_sends(up, d):
-        return jnp.logical_and(z + 1 < L, z - (d - 1) >= 0) if up else jnp.logical_and(z >= 1, z + (d - 1) < L)
-
-    def line_gets(up, d):
-        return z - d >= 0 if up else z + d < L
+    def line_sends(up, d, ci):
+        begin = z - (d - 1) if up else z + (d - 1)
+        follows = z + 1 < L if up else z >= 1
+        if ci in OTHER:
+            return jnp.logical_and(follows, begin == (0 if up else L - 1))
+        return jnp.logical_and(follows, begin >= 0 if up else begin < L)
+
+    def line_gets(up, d, ci):
+        begin = z - d if up else z + d
+        if ci in OTHER:
+            return begin == (0 if up else L - 1)
+        return begin >= 0 if up else begin < L
+
+    def inner(begin):
+        return jnp.logical_and(begin > 0, begin < L - 1)
 
     def line_got(up, d, ci):
         src, k = line_piece(z - d if up else z + d, ci)
@@ -115,11 +125,10 @@
             send_sem=ysend.at[begin, k], recv_sem=yrecv.at[begin, k],
             device_id=(row, pair), device_id_type=MESH)
 
-    for k in LINE:
-        if k != OTHER:
-            across(z, k, True).start()
-            for up in (True, False):
-                pl.when(line_sends(up, 1))(lambda up=up, k=k: line(up, 1, k, True).start())
+    for k, m in zip((LISTS,) + EARLY + LATE[1:], LATE + EARLY):
+        across(z, k, True).start()
+        for up in (True, False):
+            pl.when(line_sends(up, 1, m))(lambda up=up, m=m: line(up, 1, m, True).start())
 
     def tell(o):
         return pltpu.make_async_remote_copy(
@@ -154,19 +163,23 @@
         if o:
             give(o, row).start()
 
-    across_got(z, EARLY).wait_recv()
-    for up in (True, False):
-        pl.when(line_sends(up, 1))(lambda up=up: line(up, 1, OTHER).start())
+    for k, ci in zip(EARLY, OTHER):
+        across_got(z, k).wait_recv()
+        for up in (True, False):
+            pl.when(line_sends(up, 1, ci))(lambda up=up, ci=ci: line(up, 1, ci).start())
 
     def step(d, carry):
         for ci in LINE:
             for up in (True, False):
-                @pl.when(line_gets(up, d))
+                @pl.when(line_gets(up, d, ci))
                 def _():
+                    begin = z - d if up else z + d
                     line_got(up, d, ci).wait_recv()
-                    pl.when(line_sends(up, d + 1))(lambda: line(up, d + 1, ci).start())
+                    pl.when(line_sends(up, d + 1, ci))(lambda: line(up, d + 1, ci).start())
                     if ci in LATE:
-                        across(z - d if up else z + d, ci).start()
+                        across(begin, ci).start()
+                    elif ci in EARLY:
+                        pl.when(inner(begin))(lambda: across(begin, ci).start())
         return carry
 
     none = R * SLOTS
@@ -230,6 +243,8 @@
     def theirs(begin):
         for k in LATE[1:]:
             across_got(begin, k).wait_recv()
+        for k in EARLY:
+            pl.when(jnp.logical_and(inner(begin), begin != z))(lambda k=k: across_got(begin, k).wait_recv())
         multiply(2 * begin + 1 - y)
 
     near = min(2, L - 1)
@@ -259,14 +274,16 @@
     each(near + 1, L - 1, theirs)
 
     for begin in range(L):
+        begin = jnp.int32(begin)
         for k in LATE:
             across(begin, k).wait_send()
-    across(z, EARLY).wait_send()
+        for k in EARLY:
+            pl.when(jnp.logical_or(inner(begin), begin == z))(lambda k=k: across(begin, k).wait_send())
 
     def drain(d, carry):
         for ci in LINE:
             for up in (True, False):
-                pl.when(line_sends(up, d))(lambda up=up, ci=ci: line(up, d, ci).wait_send())
+                pl.when(line_sends(up, d, ci))(lambda up=up, ci=ci: line(up, d, ci).wait_send())
         return carry
 
     lax.fori_loop(1, L, drain, 0)
@@ -297,8 +314,8 @@
             pltpu.VMEM((1, 128), jnp.int32),
             pltpu.VMEM((N + R, 1, 128), jnp.int32),
             pltpu.SMEM((N + R, 1, 128), jnp.int32),
-            dma((2, L, PIECES + 2)),
-            dma((2, L, PIECES + 2)),
+            dma((2, L, PIECES + 1 + len(EARLY))),
+            dma((2, L, PIECES + 1 + len(EARLY))),
             dma((L, PIECES + 1)),
             dma((L, PIECES + 1)),
             dma((R,)),

time: 34.3 us -> 32.2 us (0.939)
  Pallas kernels: 32.4 us -> 30.4 us
    pallas_call x1, Pallas kernels: 32.4 us -> 30.4 us  [body(): pl.pallas_call(functools.partial(kernel, R, N), out_shape=jax.ShapeDtypeS...]
where the time goes in v3:
time: 32.2 us; the launch traced here: 32.1 us
  Pallas kernels  30.4 us (94%)
  local copies, waits for them, and re-layouts  1.67 us (5%)
    pallas_call x1, Pallas kernels, body(): pl.pallas_call(functools.partial(kernel, R, N), out_shape=jax.ShapeDtypeS...  30.4 us
    unnamed x1, local copies, waits for them, and re-layouts  1.67 us

profile of v3, /device:TPU:0, one launch (start us, length us, event | category | flops | bytes accessed | tf_op | source)
XLA Modules:
  0.0 32.1 jit_solution(2195115165457931749)
XLA Ops:
  0.0 30.4 %shard_map.64 = f32[1,1,4,128,128]{4,3,2,1,0:T(8,128)} custom-call(s32[1,1,2,2]{3,2,1,0:T(2,128)} %arows.1, s32[1,1,2,2,4]{4,3,2,1,0:T(2,128)} %bitcast.3, s32[1,1,4]{2,1,0:T(1,128)} %clist.1, f32[1,1,512,128]{3,2,1,0:T(8,128)} %bitcast.2, f32[1,1,2,4,128,128]{5,4,3,2,1,0:T(8,128)} %b_ref.1, f32[1,1,4,128,128]{4,3,2,1,0:T(8,128)} %cp_ref.1), custom_call_target="tpu_custom_call" | custom-call | tf_op jit(solution)/shard_map/pallas_call | solution.py:302
  30.4 1.7 %copy.8 = f32[1,1,4,128,128]{4,3,2,1,0:T(8,128)} copy(f32[1,1,4,128,128]{4,3,2,1,0:T(8,128)} %shard_map.64) | data formatting | bytes 524288

commit v4 on v3

--- a/solution.py
+++ b/solution.py
@@ -17,10 +17,10 @@
 BLOCKS = SECTIONS * NA
 SLOTS = SECTIONS * SLOT
 ROWS = BLOCKS * BS
-CUTS = (0, 64, 128, 320, ROWS)
+CUTS = (0, 144, 328, ROWS)
 PIECES = len(CUTS) - 1
 LISTS = PIECES
-EARLY = (0, 1)
+EARLY = (0,)
 LATE = (LISTS,) + tuple(k for k in range(PIECES) if k not in EARLY)
 OTHER = tuple(PIECES + 1 + k for k in range(len(EARLY)))
 LINE = LATE + EARLY + OTHER
@@ -63,11 +63,12 @@
     mbuf[col] = tile
     mbuf[N + row] = tile
 
+    a_in.wait()
     edge = jnp.where(z + 1 < L, 1, 0) + jnp.where(z >= 1, 1, 0)
     pl.semaphore_wait(barrier, R + edge)
 
     def own(k):
-        return mtile if k == LISTS else a_ref.at[0, 0, pl.ds(CUTS[k], CUTS[k + 1] - CUTS[k])]
+        return held(col, k)
 
     def held(src, k):
         return mbuf.at[src] if k == LISTS else abuf.at[src, pl.ds(CUTS[k], CUTS[k + 1] - CUTS[k])]
@@ -260,7 +261,6 @@
         give(o, (row - o + R) % R).wait_recv()
     lax.fori_loop(0, none + 1, split, 0)
     sides.wait()
-    a_in.wait()
     c_in.wait()
     each(0, near, mine)
     each(0, 0, theirs)

time: 32.2 us -> 31.5 us (0.978)
  Pallas kernels: 30.4 us -> 29.6 us
    pallas_call x1, Pallas kernels: 30.4 us -> 29.6 us  [body(): pl.pallas_call(functools.partial(kernel, R, N), out_shape=jax.ShapeDtypeS...]
where the time goes in v4:
time: 31.5 us; the launch traced here: 31.3 us
  Pallas kernels  29.6 us (94%)
  local copies, waits for them, and re-layouts  1.67 us (5%)
    pallas_call x1, Pallas kernels, body(): pl.pallas_call(functools.partial(kernel, R, N), out_shape=jax.ShapeDtypeS...  29.6 us
    unnamed x1, local copies, waits for them, and re-layouts  1.67 us

profile of v4, /device:TPU:0, one launch (start us, length us, event | category | flops | bytes accessed | tf_op | source)
XLA Modules:
  0.0 31.3 jit_solution(15898841560051773289)
XLA Ops:
  0.0 29.6 %shard_map.64 = f32[1,1,4,128,128]{4,3,2,1,0:T(8,128)} custom-call(s32[1,1,2,2]{3,2,1,0:T(2,128)} %arows.1, s32[1,1,2,2,4]{4,3,2,1,0:T(2,128)} %bitcast.3, s32[1,1,4]{2,1,0:T(1,128)} %clist.1, f32[1,1,512,128]{3,2,1,0:T(8,128)} %bitcast.2, f32[1,1,2,4,128,128]{5,4,3,2,1,0:T(8,128)} %b_ref.1, f32[1,1,4,128,128]{4,3,2,1,0:T(8,128)} %cp_ref.1), custom_call_target="tpu_custom_call" | custom-call | tf_op jit(solution)/shard_map/pallas_call | solution.py:302
  29.6 1.7 %copy.8 = f32[1,1,4,128,128]{4,3,2,1,0:T(8,128)} copy(f32[1,1,4,128,128]{4,3,2,1,0:T(8,128)} %shard_map.64) | data formatting | bytes 524288
